TPU v7x, 512 devices: a whole 4x4x16 slice. The times are simulated.
512 devices in a mesh: gx: 32 (over y, z_hi, x), gy: 16 (over z_lo, core).
Axes of the slice: x: 4, y: 4, z: 16 (z_hi: 2, z_lo: 8; z = z_hi * 8 + z_lo), core: 2. Of those that a mesh axis runs over, the one named last changes fastest.
Arguments:
- e_field: float32 [3, 256, 256, 128], P(None, 'gx', 'gy'), may hold values from -30 to 30
- h_field: float32 [3, 256, 256, 128], P(None, 'gx', 'gy'), may hold values from -30 to 30
- material: int32 [256, 256, 64], P('gx', 'gy'), may hold values from 0 to 3
- permittivity: float32 [4], replicated, may hold values from 1 to 12
- frequencies: float32 [4], replicated, may hold values from 0.6 to 2.4
Outputs:
- e_out: float32 [3, 256, 256, 128], P(None, 'gx', 'gy')
- h_out: float32 [3, 256, 256, 128], P(None, 'gx', 'gy')
- gram: float32 [8, 8], replicated
All inputs are finite; a program needn't handle non-finite values.
Results may differ from a plain program's by a relative error of at most 0.000096.
Values sent between devices are 32-bit elements; how exact they have to be, the bound alone decides.
No kernel may reach another device: no remote copies, remote signals or barrier semaphores. Data moves between devices by JAX's collectives and lax.ppermute only.
A program may use at most 64 MiB of HBM per device.

v0:
```python
import jax
import jax.numpy as jnp
from jax import lax
from jax.sharding import PartitionSpec as P

NZ = 64
SOURCES = 2
FILTERS = 4
MATERIALS = 4
ITERS = 4
TIME_STEP = 0.5


def from_behind(value, axis, steps):
    count = lax.axis_size(axis)
    pairs = [(source, (source + steps) % count) for source in range(count)]
    return lax.ppermute(value, axis, pairs)


def forward_z(field):
    pad = jnp.zeros(field.shape[:-1] + (SOURCES,), field.dtype)
    return jnp.concatenate([field[..., SOURCES:], pad], axis=-1) - field


def backward_z(field):
    pad = jnp.zeros(field.shape[:-1] + (SOURCES,), field.dtype)
    return field - jnp.concatenate([pad, field[..., :-SOURCES]], axis=-1)


def next_values(e_field):
    plane_x = from_behind(e_field[1:3, :1], "gx", -1)
    plane_y = from_behind(jnp.stack([e_field[0][:, :1], e_field[2][:, :1]]), "gy", -1)
    ey_next_x = jnp.concatenate([e_field[1, 1:], plane_x[0]], axis=0)
    ez_next_x = jnp.concatenate([e_field[2, 1:], plane_x[1]], axis=0)
    ex_next_y = jnp.concatenate([e_field[0][:, 1:], plane_y[0]], axis=1)
    ez_next_y = jnp.concatenate([e_field[2][:, 1:], plane_y[1]], axis=1)
    return (ey_next_x, ez_next_x, ex_next_y, ez_next_y)


def prev_values(h_field):
    plane_x = from_behind(h_field[1:3, -1:], "gx", 1)
    plane_y = from_behind(jnp.stack([h_field[0][:, -1:], h_field[2][:, -1:]]), "gy", 1)
    hy_prev_x = jnp.concatenate([plane_x[0], h_field[1, :-1]], axis=0)
    hz_prev_x = jnp.concatenate([plane_x[1], h_field[2, :-1]], axis=0)
    hx_prev_y = jnp.concatenate([plane_y[0], h_field[0][:, :-1]], axis=1)
    hz_prev_y = jnp.concatenate([plane_y[1], h_field[2][:, :-1]], axis=1)
    return (hy_prev_x, hz_prev_x, hx_prev_y, hz_prev_y)


def advance(e_field, h_field, scaled, next_fn, prev_fn):
    e_x, e_y, e_z = (e_field[0], e_field[1], e_field[2])
    ey_next_x, ez_next_x, ex_next_y, ez_next_y = next_fn(e_field)
    curl_x = ez_next_y - e_z - forward_z(e_y)
    curl_y = forward_z(e_x) - (ez_next_x - e_z)
    curl_z = ey_next_x - e_y - (ex_next_y - e_x)
    h_field = h_field - TIME_STEP * jnp.stack([curl_x, curl_y, curl_z])
    h_x, h_y, h_z = (h_field[0], h_field[1], h_field[2])
    hy_prev_x, hz_prev_x, hx_prev_y, hz_prev_y = prev_fn(h_field)
    curl_x = h_z - hz_prev_y - backward_z(h_y)
    curl_y = backward_z(h_x) - (h_z - hz_prev_x)
    curl_z = h_y - hy_prev_x - (h_x - hx_prev_y)
    e_field = jnp.stack([e_x + scaled * curl_x, e_y + scaled * curl_y, e_z + scaled * curl_z])
    return (e_field, h_field)


def body(e_field, h_field, material, permittivity, frequencies):
    onehot = (material[..., None] == jnp.arange(MATERIALS, dtype=jnp.int32)).astype(jnp.float32)
    permit_cell = jnp.sum(onehot * permittivity, axis=-1)
    permit = jnp.repeat(permit_cell, SOURCES, axis=-1)
    scaled = TIME_STEP / permit
    filtered = jnp.zeros((FILTERS,) + e_field.shape, jnp.float32)
    for step in range(ITERS):
        e_field, h_field = advance(e_field, h_field, scaled, next_values, prev_values)
        weights = jnp.cos(frequencies * ((step + 1) * TIME_STEP))
        filtered = filtered + weights[:, None, None, None, None] * e_field[None]
    count = filtered[0].size // SOURCES
    weighted = (filtered * permit[None, None]).reshape(FILTERS, count, SOURCES)
    plain = filtered.reshape(FILTERS, count, SOURCES)
    local = jnp.einsum("kms,lmt->kslt", weighted, plain, precision=lax.Precision.HIGHEST)
    local = local.reshape(FILTERS * SOURCES, FILTERS * SOURCES)
    summed = lax.psum(local, ("gx", "gy"))
    cells = e_field.shape[1] * lax.axis_size("gx") * e_field.shape[2] * lax.axis_size("gy") * NZ
    return (e_field, h_field, summed / cells)


def solution(mesh):
    in_specs = (P(None, "gx", "gy", None), P(None, "gx", "gy", None), P("gx", "gy", None), P(), P())
    out_specs = (P(None, "gx", "gy", None), P(None, "gx", "gy", None), P())
    return jax.shard_map(body, mesh=mesh, in_specs=in_specs, out_specs=out_specs, check_vma=False)
```

profile of v0, /device:TPU:1, one launch (start us, length us, event | category | flops | bytes accessed | tf_op | source)
XLA Modules:
  0.0 369.0 jit_solution(447718432147306307)
XLA Ops:
  0.6 0.7 slice.390
  1.4 20.9 %collective-permute-start.1 = (f32[2,1,16,128]{3,2,1,0:T(8,128)S(1)}, f32[2,1,16,128]{3,2,1,0:T(8,128)S(1)}, u32[]{:S(2)}, u32[]{:S(2)}) collective-permute-start(f32[2,1,16,128]{3,2,1,0:T(8,128)S(1)} %slice.390), channel_id=1, source_target_pairs={{0,496},{16,0},{32,16},{48,32},{64,48},{80,64},{96,80},{112,96},{1... | collective-permute-start | bytes 49160 | tf_op jit(solution)/shard_map/ppermute | solution.py:17
  22.3 0.9 slice_bitcast_fusion.16
  23.2 2.9 collective-permute-start
  26.1 0.9 slice_bitcast_fusion.27
  26.9 1.0 select_reduce_fusion
  27.9 0.7 multiply_cosine_fusion.2
  28.7 0.1 slice.504
  28.8 0.2 copy.751
  28.9 0.1 copy.759
  29.1 0.2 copy.760
  29.4 0.2 copy.752
  29.6 14.0 %mul.282 = f32[24576,2]{1,0:T(8,128)} reshape(f32[3,8,16,128]{3,2,1,0:T(8,128)S(1)} %mul.281) | data formatting | bytes 393216 | tf_op jit(solution)/shard_map/mul | solution.py:77
  43.6 7.5 %copy.782 = f32[2,24576]{1,0:T(2,128)S(1)} copy(f32[2,24576]{0,1:T(8,128)} %bitcast.290) | data formatting | bytes 393216 | tf_op jit(solution)/shard_map/mul | solution.py:77
  51.2 0.1 slice.503
  51.5 2.7 collective-permute-start.2
  54.2 1.9 collective-permute-start.3
  56.2 0.8 collective-permute-done.2
  57.0 14.7 %collective-permute-done.3 = f32[2,1,16,128]{3,2,1,0:T(8,128)S(1)} collective-permute-done((f32[2,1,16,128]{3,2,1,0:T(8,128)S(1)}, f32[2,1,16,128]{3,2,1,0:T(8,128)S(1)}, u32[]{:S(2)}, u32[]{:S(2)}) %collective-permute-start.3) | collective-permute-done | bytes 16416 | tf_op jit(solution)/shard_map/ppermute | solution.py:17
  71.7 0.1 fusion.11
  71.8 1.9 collective-permute-start.5
  73.8 0.1 slice.530
  73.9 2.5 collective-permute-done.5
  76.4 6.3 %collective-permute-start.4 = (f32[2,8,1,128]{3,1,2,0:T(8,128)S(1)}, f32[2,8,1,128]{3,1,2,0:T(8,128)S(1)}, u32[]{:S(2)}, u32[]{:S(2)}) collective-permute-start(f32[2,8,1,128]{3,1,2,0:T(8,128)S(1)} %pad_maximum_fusion.9), channel_id=1, source_target_pairs={{0,15},{1,0},{2,1},{3,2},{4,3},{5,4},{6,5},{7,6},{8,7},{9,8},{10,9... | collective-permute-start | bytes 24584 | tf_op jit(solution)/shard_map/ppermute | solution.py:17
  82.8 0.1 slice.529
  82.9 14.0 %mul.260 = f32[24576,2]{1,0:T(8,128)} reshape(f32[3,8,16,128]{3,2,1,0:T(8,128)S(1)} %pad_maximum_fusion.1) | data formatting | bytes 393216 | tf_op jit(solution)/shard_map/mul | solution.py:75
  96.9 7.5 %copy.777 = f32[2,24576]{1,0:T(2,128)S(1)} copy(f32[2,24576]{0,1:T(8,128)} %bitcast.291) | data formatting | bytes 393216 | tf_op jit(solution)/shard_map/mul | solution.py:75
  104.6 1.9 collective-permute-start.6
  106.6 1.9 collective-permute-start.7
  108.5 4.7 %collective-permute-done.6 = f32[2,8,1,128]{3,1,2,0:T(8,128)S(1)} collective-permute-done((f32[2,8,1,128]{3,1,2,0:T(8,128)S(1)}, f32[2,8,1,128]{3,1,2,0:T(8,128)S(1)}, u32[]{:S(2)}, u32[]{:S(2)}) %collective-permute-start.6) | collective-permute-done | bytes 8224 | tf_op jit(solution)/shard_map/ppermute | solution.py:17
  113.2 10.8 %collective-permute-done.7 = f32[2,1,16,128]{3,2,1,0:T(8,128)S(1)} collective-permute-done((f32[2,1,16,128]{3,2,1,0:T(8,128)S(1)}, f32[2,1,16,128]{3,2,1,0:T(8,128)S(1)}, u32[]{:S(2)}, u32[]{:S(2)}) %collective-permute-start.7) | collective-permute-done | bytes 16416 | tf_op jit(solution)/shard_map/ppermute | solution.py:17
  124.0 0.1 fusion.29
  124.2 4.1 %collective-permute-start.9 = (f32[2,1,16,128]{3,2,1,0:T(8,128)S(1)}, f32[2,1,16,128]{3,2,1,0:T(8,128)S(1)}, u32[]{:S(2)}, u32[]{:S(2)}) collective-permute-start(f32[2,1,16,128]{3,2,1,0:T(8,128)S(1)} %pad_maximum_fusion.5), channel_id=1, source_target_pairs={{0,496},{16,0},{32,16},{48,32},{64,48},{80,64},{96,80},{112,96},{1... | collective-permute-start | bytes 49160 | tf_op jit(solution)/shard_map/ppermute | solution.py:17
  128.3 0.1 slice.558
  128.4 0.7 collective-permute-done.9
  129.2 11.8 %collective-permute-start.8 = (f32[2,8,1,128]{3,1,2,0:T(8,128)S(1)}, f32[2,8,1,128]{3,1,2,0:T(8,128)S(1)}, u32[]{:S(2)}, u32[]{:S(2)}) collective-permute-start(f32[2,8,1,128]{3,1,2,0:T(8,128)S(1)} %pad_maximum_fusion.11), channel_id=1, source_target_pairs={{0,15},{1,0},{2,1},{3,2},{4,3},{5,4},{6,5},{7,6},{8,7},{9,8},{10,9... | collective-permute-start | bytes 24584 | tf_op jit(solution)/shard_map/ppermute | solution.py:17
  141.0 0.1 slice.557
  141.1 14.0 %mul.265 = f32[24576,2]{1,0:T(8,128)} reshape(f32[3,8,16,128]{3,2,1,0:T(8,128)S(1)} %pad_maximum_fusion.2) | data formatting | bytes 393216 | tf_op jit(solution)/shard_map/mul | solution.py:75
  155.1 7.5 %copy.778 = f32[2,24576]{1,0:T(2,128)S(1)} copy(f32[2,24576]{0,1:T(8,128)} %bitcast.292) | data formatting | bytes 393216 | tf_op jit(solution)/shard_map/mul | solution.py:75
  162.9 1.9 collective-permute-start.10
  164.9 1.9 collective-permute-start.11
  166.8 2.7 collective-permute-done.10
  169.5 13.3 %collective-permute-done.11 = f32[2,1,16,128]{3,2,1,0:T(8,128)S(1)} collective-permute-done((f32[2,1,16,128]{3,2,1,0:T(8,128)S(1)}, f32[2,1,16,128]{3,2,1,0:T(8,128)S(1)}, u32[]{:S(2)}, u32[]{:S(2)}) %collective-permute-start.11) | collective-permute-done | bytes 16416 | tf_op jit(solution)/shard_map/ppermute | solution.py:17
  182.9 0.1 fusion.47
  183.0 3.4 collective-permute-start.13
  186.4 0.1 slice.586
  186.5 1.0 collective-permute-done.13
  187.6 9.7 %collective-permute-start.12 = (f32[2,8,1,128]{3,1,2,0:T(8,128)S(1)}, f32[2,8,1,128]{3,1,2,0:T(8,128)S(1)}, u32[]{:S(2)}, u32[]{:S(2)}) collective-permute-start(f32[2,8,1,128]{3,1,2,0:T(8,128)S(1)} %pad_maximum_fusion.13), channel_id=1, source_target_pairs={{0,15},{1,0},{2,1},{3,2},{4,3},{5,4},{6,5},{7,6},{8,7},{9,8},{10,9... | collective-permute-start | bytes 24584 | tf_op jit(solution)/shard_map/ppermute | solution.py:17
  197.3 0.1 slice.585
  197.4 14.0 %mul.271 = f32[24576,2]{1,0:T(8,128)} reshape(f32[3,8,16,128]{3,2,1,0:T(8,128)S(1)} %pad_maximum_fusion.3) | data formatting | bytes 393216 | tf_op jit(solution)/shard_map/mul | solution.py:75
  211.4 7.5 %copy.779 = f32[2,24576]{1,0:T(2,128)S(1)} copy(f32[2,24576]{0,1:T(8,128)} %bitcast.293) | data formatting | bytes 393216 | tf_op jit(solution)/shard_map/mul | solution.py:75
  219.2 1.9 collective-permute-start.14
  221.2 2.1 collective-permute-start.15
  223.3 2.5 collective-permute-done.14
  225.8 13.4 %collective-permute-done.15 = f32[2,1,16,128]{3,2,1,0:T(8,128)S(1)} collective-permute-done((f32[2,1,16,128]{3,2,1,0:T(8,128)S(1)}, f32[2,1,16,128]{3,2,1,0:T(8,128)S(1)}, u32[]{:S(2)}, u32[]{:S(2)}) %collective-permute-start.15) | collective-permute-done | bytes 16416 | tf_op jit(solution)/shard_map/ppermute | solution.py:17
  239.2 0.1 fusion.66
  239.3 14.0 %mul.277 = f32[24576,2]{1,0:T(8,128)} reshape(f32[3,8,16,128]{3,2,1,0:T(8,128)S(1)} %pad_maximum_fusion) | data formatting | bytes 393216 | tf_op jit(solution)/shard_map/mul | solution.py:75
  253.3 7.5 %copy.780 = f32[2,24576]{1,0:T(2,128)S(1)} copy(f32[2,24576]{0,1:T(8,128)} %bitcast.294) | data formatting | bytes 393216 | tf_op jit(solution)/shard_map/mul | solution.py:75
  260.9 0.9 broadcast_multiply_fusion
  261.9 0.5 mul.286
  262.4 0.5 add.163
  263.0 1.9 fusion.85
  264.8 103.5 %psum.7 = f32[8,8]{1,0:T(8,128)S(1)} all-reduce(f32[8,8]{1,0:T(8,128)S(1)} %fusion.85), channel_id=1, replica_groups=mesh['gx'=32,'gy'=16] {'gx','gy'}, use_global_device_ids=true, to_apply=%region_1.0 | all-reduce | flops 64 | bytes 512 | tf_op jit(solution)/shard_map/psum | solution.py:81
  368.4 0.6 broadcast_multiply_fusion.1
  (113 shorter events, 1.4 us)
Async XLA Ops:
  1.4 49.8 %collective-permute-start.1 = (f32[2,1,16,128]{3,2,1,0:T(8,128)S(1)}, f32[2,1,16,128]{3,2,1,0:T(8,128)S(1)}, u32[]{:S(2)}, u32[]{:S(2)}) collective-permute-start(f32[2,1,16,128]{3,2,1,0:T(8,128)S(1)} %slice.390), channel_id=1, source_target_pairs={{0,496},{16,0},{32,16},{48,32},{64,48},{80,64},{96,80},{112,96},{1... | collective-permute-start | bytes 49160 | tf_op jit(solution)/shard_map/ppermute | solution.py:17
  23.2 28.0 %collective-permute-start = (f32[2,8,1,128]{3,1,2,0:T(8,128)S(1)}, f32[2,8,1,128]{3,1,2,0:T(8,128)S(1)}, u32[]{:S(2)}, u32[]{:S(2)}) collective-permute-start(f32[2,8,1,128]{3,1,2,0:T(8,128)S(1)} %pad_maximum_fusion.7), channel_id=1, source_target_pairs={{0,15},{1,0},{2,1},{3,2},{4,3},{5,4},{6,5},{7,6},{8,7},{9,8},{10,9... | collective-permute-start | bytes 24584 | tf_op jit(solution)/shard_map/ppermute | solution.py:17
  29.6 21.6 %copy-start = (f32[3,8,16,128]{3,2,1,0:T(8,128)S(1)}, f32[3,8,16,128]{3,2,1,0:T(8,128)}, u32[]{:S(2)}) copy-start(f32[3,8,16,128]{3,2,1,0:T(8,128)} %param.5) | copy-start | bytes 589828
  29.6 21.8 %copy-start.2 = (f32[3,8,16,128]{3,2,1,0:T(8,128)S(1)}, f32[3,8,16,128]{3,2,1,0:T(8,128)}, u32[]{:S(2)}) copy-start(f32[3,8,16,128]{3,2,1,0:T(8,128)} %param.6) | copy-start | bytes 589828
  51.5 5.5 %collective-permute-start.2 = (f32[2,8,1,128]{3,1,2,0:T(8,128)S(1)}, f32[2,8,1,128]{3,1,2,0:T(8,128)S(1)}, u32[]{:S(2)}, u32[]{:S(2)}) collective-permute-start(f32[2,8,1,128]{3,1,2,0:T(8,128)S(1)} %pad_maximum_fusion.8), channel_id=1, source_target_pairs={{0,1},{1,2},{2,3},{3,4},{4,5},{5,6},{6,7},{7,8},{8,9},{9,10},{10,1... | collective-permute-start | bytes 24584 | tf_op jit(solution)/shard_map/ppermute | solution.py:17
  54.2 17.4 %collective-permute-start.3 = (f32[2,1,16,128]{3,2,1,0:T(8,128)S(1)}, f32[2,1,16,128]{3,2,1,0:T(8,128)S(1)}, u32[]{:S(2)}, u32[]{:S(2)}) collective-permute-start(f32[2,1,16,128]{3,2,1,0:T(8,128)S(1)} %slice.517), channel_id=1, source_target_pairs={{0,16},{16,32},{32,48},{48,64},{64,80},{80,96},{96,112},{112,128},... | collective-permute-start | bytes 49160 | tf_op jit(solution)/shard_map/ppermute | solution.py:17
  71.8 4.5 %collective-permute-start.5 = (f32[2,1,16,128]{3,2,1,0:T(8,128)S(1)}, f32[2,1,16,128]{3,2,1,0:T(8,128)S(1)}, u32[]{:S(2)}, u32[]{:S(2)}) collective-permute-start(f32[2,1,16,128]{3,2,1,0:T(8,128)S(1)} %pad_maximum_fusion.6), channel_id=1, source_target_pairs={{0,496},{16,0},{32,16},{48,32},{64,48},{80,64},{96,80},{112,96},{1... | collective-permute-start | bytes 49160 | tf_op jit(solution)/shard_map/ppermute | solution.py:17
  76.4 28.0 %collective-permute-start.4 = (f32[2,8,1,128]{3,1,2,0:T(8,128)S(1)}, f32[2,8,1,128]{3,1,2,0:T(8,128)S(1)}, u32[]{:S(2)}, u32[]{:S(2)}) collective-permute-start(f32[2,8,1,128]{3,1,2,0:T(8,128)S(1)} %pad_maximum_fusion.9), channel_id=1, source_target_pairs={{0,15},{1,0},{2,1},{3,2},{4,3},{5,4},{6,5},{7,6},{8,7},{9,8},{10,9... | collective-permute-start | bytes 24584 | tf_op jit(solution)/shard_map/ppermute | solution.py:17
  104.6 8.6 %collective-permute-start.6 = (f32[2,8,1,128]{3,1,2,0:T(8,128)S(1)}, f32[2,8,1,128]{3,1,2,0:T(8,128)S(1)}, u32[]{:S(2)}, u32[]{:S(2)}) collective-permute-start(f32[2,8,1,128]{3,1,2,0:T(8,128)S(1)} %pad_maximum_fusion.10), channel_id=1, source_target_pairs={{0,1},{1,2},{2,3},{3,4},{4,5},{5,6},{6,7},{7,8},{8,9},{9,10},{10,1... | collective-permute-start | bytes 24584 | tf_op jit(solution)/shard_map/ppermute | solution.py:17
  106.6 17.4 %collective-permute-start.7 = (f32[2,1,16,128]{3,2,1,0:T(8,128)S(1)}, f32[2,1,16,128]{3,2,1,0:T(8,128)S(1)}, u32[]{:S(2)}, u32[]{:S(2)}) collective-permute-start(f32[2,1,16,128]{3,2,1,0:T(8,128)S(1)} %slice.545), channel_id=1, source_target_pairs={{0,16},{16,32},{32,48},{48,64},{64,80},{80,96},{96,112},{112,128},... | collective-permute-start | bytes 49160 | tf_op jit(solution)/shard_map/ppermute | solution.py:17
  124.2 5.0 %collective-permute-start.9 = (f32[2,1,16,128]{3,2,1,0:T(8,128)S(1)}, f32[2,1,16,128]{3,2,1,0:T(8,128)S(1)}, u32[]{:S(2)}, u32[]{:S(2)}) collective-permute-start(f32[2,1,16,128]{3,2,1,0:T(8,128)S(1)} %pad_maximum_fusion.5), channel_id=1, source_target_pairs={{0,496},{16,0},{32,16},{48,32},{64,48},{80,64},{96,80},{112,96},{1... | collective-permute-start | bytes 49160 | tf_op jit(solution)/shard_map/ppermute | solution.py:17
  129.2 33.5 %collective-permute-start.8 = (f32[2,8,1,128]{3,1,2,0:T(8,128)S(1)}, f32[2,8,1,128]{3,1,2,0:T(8,128)S(1)}, u32[]{:S(2)}, u32[]{:S(2)}) collective-permute-start(f32[2,8,1,128]{3,1,2,0:T(8,128)S(1)} %pad_maximum_fusion.11), channel_id=1, source_target_pairs={{0,15},{1,0},{2,1},{3,2},{4,3},{5,4},{6,5},{7,6},{8,7},{9,8},{10,9... | collective-permute-start | bytes 24584 | tf_op jit(solution)/shard_map/ppermute | solution.py:17
  162.9 6.6 %collective-permute-start.10 = (f32[2,8,1,128]{3,1,2,0:T(8,128)S(1)}, f32[2,8,1,128]{3,1,2,0:T(8,128)S(1)}, u32[]{:S(2)}, u32[]{:S(2)}) collective-permute-start(f32[2,8,1,128]{3,1,2,0:T(8,128)S(1)} %pad_maximum_fusion.12), channel_id=1, source_target_pairs={{0,1},{1,2},{2,3},{3,4},{4,5},{5,6},{6,7},{7,8},{8,9},{9,10},{10,1... | collective-permute-start | bytes 24584 | tf_op jit(solution)/shard_map/ppermute | solution.py:17
  164.9 18.0 %collective-permute-start.11 = (f32[2,1,16,128]{3,2,1,0:T(8,128)S(1)}, f32[2,1,16,128]{3,2,1,0:T(8,128)S(1)}, u32[]{:S(2)}, u32[]{:S(2)}) collective-permute-start(f32[2,1,16,128]{3,2,1,0:T(8,128)S(1)} %slice.573), channel_id=1, source_target_pairs={{0,16},{16,32},{32,48},{48,64},{64,80},{80,96},{96,112},{112,128},... | collective-permute-start | bytes 49160 | tf_op jit(solution)/shard_map/ppermute | solution.py:17
  183.0 4.5 %collective-permute-start.13 = (f32[2,1,16,128]{3,2,1,0:T(8,128)S(1)}, f32[2,1,16,128]{3,2,1,0:T(8,128)S(1)}, u32[]{:S(2)}, u32[]{:S(2)}) collective-permute-start(f32[2,1,16,128]{3,2,1,0:T(8,128)S(1)} %pad_maximum_fusion.4), channel_id=1, source_target_pairs={{0,496},{16,0},{32,16},{48,32},{64,48},{80,64},{96,80},{112,96},{1... | collective-permute-start | bytes 49160 | tf_op jit(solution)/shard_map/ppermute | solution.py:17
  187.6 31.4 %collective-permute-start.12 = (f32[2,8,1,128]{3,1,2,0:T(8,128)S(1)}, f32[2,8,1,128]{3,1,2,0:T(8,128)S(1)}, u32[]{:S(2)}, u32[]{:S(2)}) collective-permute-start(f32[2,8,1,128]{3,1,2,0:T(8,128)S(1)} %pad_maximum_fusion.13), channel_id=1, source_target_pairs={{0,15},{1,0},{2,1},{3,2},{4,3},{5,4},{6,5},{7,6},{8,7},{9,8},{10,9... | collective-permute-start | bytes 24584 | tf_op jit(solution)/shard_map/ppermute | solution.py:17
  219.1 41.8 %copy-start.1 = (f32[3,8,16,128]{3,2,1,0:T(8,128)}, f32[3,8,16,128]{3,2,1,0:T(8,128)S(1)}, u32[]{:S(2)}) copy-start(f32[3,8,16,128]{3,2,1,0:T(8,128)S(1)} %fusion.3) | copy-start | bytes 589828
  219.2 6.6 %collective-permute-start.14 = (f32[2,8,1,128]{3,1,2,0:T(8,128)S(1)}, f32[2,8,1,128]{3,1,2,0:T(8,128)S(1)}, u32[]{:S(2)}, u32[]{:S(2)}) collective-permute-start(f32[2,8,1,128]{3,1,2,0:T(8,128)S(1)} %pad_maximum_fusion.14), channel_id=1, source_target_pairs={{0,1},{1,2},{2,3},{3,4},{4,5},{5,6},{6,7},{7,8},{8,9},{9,10},{10,1... | collective-permute-start | bytes 24584 | tf_op jit(solution)/shard_map/ppermute | solution.py:17
  221.2 18.0 %collective-permute-start.15 = (f32[2,1,16,128]{3,2,1,0:T(8,128)S(1)}, f32[2,1,16,128]{3,2,1,0:T(8,128)S(1)}, u32[]{:S(2)}, u32[]{:S(2)}) collective-permute-start(f32[2,1,16,128]{3,2,1,0:T(8,128)S(1)} %slice.602), channel_id=1, source_target_pairs={{0,16},{16,32},{32,48},{48,64},{64,80},{80,96},{96,112},{112,128},... | collective-permute-start | bytes 49160 | tf_op jit(solution)/shard_map/ppermute | solution.py:17
  239.3 21.6 %copy-start.3 = (f32[3,8,16,128]{3,2,1,0:T(8,128)}, f32[3,8,16,128]{3,2,1,0:T(8,128)S(1)}, u32[]{:S(2)}) copy-start(f32[3,8,16,128]{3,2,1,0:T(8,128)S(1)} %pad_maximum_fusion) | copy-start | bytes 589828
where the time goes:
time: 370 us; the launch traced here: 369 us
  local copies, waits for them, and re-layouts  113 us (31%)
  blocking collectives  104 us (28%)
  starting transfers between devices  77.3 us (21%)
  waiting for transfers between devices  67.1 us (18%)
  other arithmetic  4.46 us (1%)
    psum x1, blocking collectives, body(): summed = lax.psum(local, ('gx', 'gy'))  104 us
    mul x8, local copies, waits for them, and re-layouts, body(): filtered = filtered + weights[:, None, None, None, None] * e_field[None]  86.2 us
    ppermute x16, starting transfers between devices, from_behind(): return lax.ppermute(value, axis, pairs)  77.3 us
    ppermute x16, waiting for transfers between devices, from_behind(): return lax.ppermute(value, axis, pairs)  67.1 us
    mul x4, local copies, waits for them, and re-layouts, body(): weighted = (filtered * permit[None, None]).reshape(FILTERS, count, SOURCES)  22.1 us
  transfers between devices with their start and end apart: 16, of which 11 were waited for; matrix products, arithmetic and copies ran while one was open for 25% of the time, Pallas kernels for 0%

commit v1 on v0

--- a/solution.py
+++ b/solution.py
@@ -78,7 +78,7 @@
     plain = filtered.reshape(FILTERS, count, SOURCES)
     local = jnp.einsum("kms,lmt->kslt", weighted, plain, precision=lax.Precision.HIGHEST)
     local = local.reshape(FILTERS * SOURCES, FILTERS * SOURCES)
-    summed = lax.psum(local, ("gx", "gy"))
+    summed = lax.psum(lax.psum(local, "gy"), "gx")
     cells = e_field.shape[1] * lax.axis_size("gx") * e_field.shape[2] * lax.axis_size("gy") * NZ
     return (e_field, h_field, summed / cells)
 

time: 370 us -> 469 us (1.27)
  the two profiles are of different devices: /device:TPU:1 before, /device:TPU:2 now
where the time goes in v1:
time: 469 us; the launch traced here: 468 us
  blocking collectives  210 us (45%)
  local copies, waits for them, and re-layouts  113 us (24%)
  starting transfers between devices  99 us (21%)
  waiting for transfers between devices  38 us (8%)
    psum x2, blocking collectives, body(): summed = lax.psum(lax.psum(local, 'gy'), 'gx')  210 us
    ppermute x16, starting transfers between devices, from_behind(): return lax.ppermute(value, axis, pairs)  99 us
    mul x8, local copies, waits for them, and re-layouts, body(): filtered = filtered + weights[:, None, None, None, None] * e_field[None]  86.1 us
    ppermute x16, waiting for transfers between devices, from_behind(): return lax.ppermute(value, axis, pairs)  38 us
    mul x4, local copies, waits for them, and re-layouts, body(): weighted = (filtered * permit[None, None]).reshape(FILTERS, count, SOURCES)  22.1 us
  transfers between devices with their start and end apart: 16, of which 8 were waited for; matrix products, arithmetic and copies ran while one was open for 19% of the time, Pallas kernels for 0%

profile of v1, /device:TPU:2, one launch (start us, length us, event | category | flops | bytes accessed | tf_op | source)
XLA Modules:
  0.0 467.9 jit_solution(8295340403576753965)
XLA Ops:
  0.6 0.7 slice.390
  1.4 7.8 %collective-permute-start.1 = (f32[2,1,16,128]{3,2,1,0:T(8,128)S(1)}, f32[2,1,16,128]{3,2,1,0:T(8,128)S(1)}, u32[]{:S(2)}, u32[]{:S(2)}) collective-permute-start(f32[2,1,16,128]{3,2,1,0:T(8,128)S(1)} %slice.390), channel_id=1, source_target_pairs={{0,496},{16,0},{32,16},{48,32},{64,48},{80,64},{96,80},{112,96},{1... | collective-permute-start | bytes 49160 | tf_op jit(solution)/shard_map/ppermute | solution.py:17
  9.2 0.9 slice_bitcast_fusion.16
  10.1 6.9 %collective-permute-start = (f32[2,8,1,128]{3,1,2,0:T(8,128)S(1)}, f32[2,8,1,128]{3,1,2,0:T(8,128)S(1)}, u32[]{:S(2)}, u32[]{:S(2)}) collective-permute-start(f32[2,8,1,128]{3,1,2,0:T(8,128)S(1)} %pad_maximum_fusion.7), channel_id=1, source_target_pairs={{0,15},{1,0},{2,1},{3,2},{4,3},{5,4},{6,5},{7,6},{8,7},{9,8},{10,9... | collective-permute-start | bytes 24584 | tf_op jit(solution)/shard_map/ppermute | solution.py:17
  17.0 0.9 slice_bitcast_fusion.27
  17.9 1.0 select_reduce_fusion
  18.9 0.7 multiply_cosine_fusion.2
  19.7 0.1 slice.504
  19.7 0.2 copy.751
  19.9 0.1 copy.759
  20.1 0.2 copy.760
  20.3 0.2 copy.752
  20.6 14.0 %mul.282 = f32[24576,2]{1,0:T(8,128)} reshape(f32[3,8,16,128]{3,2,1,0:T(8,128)S(1)} %mul.281) | data formatting | bytes 393216 | tf_op jit(solution)/shard_map/mul | solution.py:77
  34.6 7.5 %copy.782 = f32[2,24576]{1,0:T(2,128)S(1)} copy(f32[2,24576]{0,1:T(8,128)} %bitcast.290) | data formatting | bytes 393216 | tf_op jit(solution)/shard_map/mul | solution.py:77
  42.2 0.1 slice.503
  42.5 1.9 collective-permute-start.2
  44.4 3.4 collective-permute-start.3
  47.8 6.2 %collective-permute-done.2 = f32[2,8,1,128]{3,1,2,0:T(8,128)S(1)} collective-permute-done((f32[2,8,1,128]{3,1,2,0:T(8,128)S(1)}, f32[2,8,1,128]{3,1,2,0:T(8,128)S(1)}, u32[]{:S(2)}, u32[]{:S(2)}) %collective-permute-start.2) | collective-permute-done | bytes 8224 | tf_op jit(solution)/shard_map/ppermute | solution.py:17
  54.1 4.9 %collective-permute-done.3 = f32[2,1,16,128]{3,2,1,0:T(8,128)S(1)} collective-permute-done((f32[2,1,16,128]{3,2,1,0:T(8,128)S(1)}, f32[2,1,16,128]{3,2,1,0:T(8,128)S(1)}, u32[]{:S(2)}, u32[]{:S(2)}) %collective-permute-start.3) | collective-permute-done | bytes 16416 | tf_op jit(solution)/shard_map/ppermute | solution.py:17
  59.1 0.1 fusion.11
  59.2 16.9 %collective-permute-start.5 = (f32[2,1,16,128]{3,2,1,0:T(8,128)S(1)}, f32[2,1,16,128]{3,2,1,0:T(8,128)S(1)}, u32[]{:S(2)}, u32[]{:S(2)}) collective-permute-start(f32[2,1,16,128]{3,2,1,0:T(8,128)S(1)} %pad_maximum_fusion.6), channel_id=1, source_target_pairs={{0,496},{16,0},{32,16},{48,32},{64,48},{80,64},{96,80},{112,96},{1... | collective-permute-start | bytes 49160 | tf_op jit(solution)/shard_map/ppermute | solution.py:17
  76.1 0.1 slice.530
  76.2 1.3 collective-permute-done.5
  77.6 8.2 %collective-permute-start.4 = (f32[2,8,1,128]{3,1,2,0:T(8,128)S(1)}, f32[2,8,1,128]{3,1,2,0:T(8,128)S(1)}, u32[]{:S(2)}, u32[]{:S(2)}) collective-permute-start(f32[2,8,1,128]{3,1,2,0:T(8,128)S(1)} %pad_maximum_fusion.9), channel_id=1, source_target_pairs={{0,15},{1,0},{2,1},{3,2},{4,3},{5,4},{6,5},{7,6},{8,7},{9,8},{10,9... | collective-permute-start | bytes 24584 | tf_op jit(solution)/shard_map/ppermute | solution.py:17
  85.8 0.1 slice.529
  85.9 14.0 %mul.260 = f32[24576,2]{1,0:T(8,128)} reshape(f32[3,8,16,128]{3,2,1,0:T(8,128)S(1)} %pad_maximum_fusion.1) | data formatting | bytes 393216 | tf_op jit(solution)/shard_map/mul | solution.py:75
  99.9 7.5 %copy.777 = f32[2,24576]{1,0:T(2,128)S(1)} copy(f32[2,24576]{0,1:T(8,128)} %bitcast.291) | data formatting | bytes 393216 | tf_op jit(solution)/shard_map/mul | solution.py:75
  107.7 1.9 collective-permute-start.6
  109.6 1.9 collective-permute-start.7
  111.6 7.7 %collective-permute-done.6 = f32[2,8,1,128]{3,1,2,0:T(8,128)S(1)} collective-permute-done((f32[2,8,1,128]{3,1,2,0:T(8,128)S(1)}, f32[2,8,1,128]{3,1,2,0:T(8,128)S(1)}, u32[]{:S(2)}, u32[]{:S(2)}) %collective-permute-start.6) | collective-permute-done | bytes 8224 | tf_op jit(solution)/shard_map/ppermute | solution.py:17
  119.3 0.1 fusion.29
  119.5 12.8 %collective-permute-start.9 = (f32[2,1,16,128]{3,2,1,0:T(8,128)S(1)}, f32[2,1,16,128]{3,2,1,0:T(8,128)S(1)}, u32[]{:S(2)}, u32[]{:S(2)}) collective-permute-start(f32[2,1,16,128]{3,2,1,0:T(8,128)S(1)} %pad_maximum_fusion.5), channel_id=1, source_target_pairs={{0,496},{16,0},{32,16},{48,32},{64,48},{80,64},{96,80},{112,96},{1... | collective-permute-start | bytes 49160 | tf_op jit(solution)/shard_map/ppermute | solution.py:17
  132.3 0.1 slice.558
  132.4 1.3 collective-permute-done.9
  133.8 8.2 %collective-permute-start.8 = (f32[2,8,1,128]{3,1,2,0:T(8,128)S(1)}, f32[2,8,1,128]{3,1,2,0:T(8,128)S(1)}, u32[]{:S(2)}, u32[]{:S(2)}) collective-permute-start(f32[2,8,1,128]{3,1,2,0:T(8,128)S(1)} %pad_maximum_fusion.11), channel_id=1, source_target_pairs={{0,15},{1,0},{2,1},{3,2},{4,3},{5,4},{6,5},{7,6},{8,7},{9,8},{10,9... | collective-permute-start | bytes 24584 | tf_op jit(solution)/shard_map/ppermute | solution.py:17
  142.1 0.1 slice.557
  142.2 14.0 %mul.265 = f32[24576,2]{1,0:T(8,128)} reshape(f32[3,8,16,128]{3,2,1,0:T(8,128)S(1)} %pad_maximum_fusion.2) | data formatting | bytes 393216 | tf_op jit(solution)/shard_map/mul | solution.py:75
  156.2 7.5 %copy.778 = f32[2,24576]{1,0:T(2,128)S(1)} copy(f32[2,24576]{0,1:T(8,128)} %bitcast.292) | data formatting | bytes 393216 | tf_op jit(solution)/shard_map/mul | solution.py:75
  163.8 0.1 fusion.2
  164.0 1.9 collective-permute-start.10
  165.9 1.9 collective-permute-start.11
  167.8 7.7 %collective-permute-done.10 = f32[2,8,1,128]{3,1,2,0:T(8,128)S(1)} collective-permute-done((f32[2,8,1,128]{3,1,2,0:T(8,128)S(1)}, f32[2,8,1,128]{3,1,2,0:T(8,128)S(1)}, u32[]{:S(2)}, u32[]{:S(2)}) %collective-permute-start.10) | collective-permute-done | bytes 8224 | tf_op jit(solution)/shard_map/ppermute | solution.py:17
  175.6 0.1 fusion.47
  175.7 12.8 %collective-permute-start.13 = (f32[2,1,16,128]{3,2,1,0:T(8,128)S(1)}, f32[2,1,16,128]{3,2,1,0:T(8,128)S(1)}, u32[]{:S(2)}, u32[]{:S(2)}) collective-permute-start(f32[2,1,16,128]{3,2,1,0:T(8,128)S(1)} %pad_maximum_fusion.4), channel_id=1, source_target_pairs={{0,496},{16,0},{32,16},{48,32},{64,48},{80,64},{96,80},{112,96},{1... | collective-permute-start | bytes 49160 | tf_op jit(solution)/shard_map/ppermute | solution.py:17
  188.6 0.1 slice.586
  188.7 1.3 collective-permute-done.13
  190.1 8.2 %collective-permute-start.12 = (f32[2,8,1,128]{3,1,2,0:T(8,128)S(1)}, f32[2,8,1,128]{3,1,2,0:T(8,128)S(1)}, u32[]{:S(2)}, u32[]{:S(2)}) collective-permute-start(f32[2,8,1,128]{3,1,2,0:T(8,128)S(1)} %pad_maximum_fusion.13), channel_id=1, source_target_pairs={{0,15},{1,0},{2,1},{3,2},{4,3},{5,4},{6,5},{7,6},{8,7},{9,8},{10,9... | collective-permute-start | bytes 24584 | tf_op jit(solution)/shard_map/ppermute | solution.py:17
  198.4 0.1 slice.585
  198.5 14.0 %mul.271 = f32[24576,2]{1,0:T(8,128)} reshape(f32[3,8,16,128]{3,2,1,0:T(8,128)S(1)} %pad_maximum_fusion.3) | data formatting | bytes 393216 | tf_op jit(solution)/shard_map/mul | solution.py:75
  212.4 7.5 %copy.779 = f32[2,24576]{1,0:T(2,128)S(1)} copy(f32[2,24576]{0,1:T(8,128)} %bitcast.293) | data formatting | bytes 393216 | tf_op jit(solution)/shard_map/mul | solution.py:75
  220.1 0.1 fusion.3
  220.2 1.9 collective-permute-start.14
  222.2 2.1 collective-permute-start.15
  224.3 7.5 %collective-permute-done.14 = f32[2,8,1,128]{3,1,2,0:T(8,128)S(1)} collective-permute-done((f32[2,8,1,128]{3,1,2,0:T(8,128)S(1)}, f32[2,8,1,128]{3,1,2,0:T(8,128)S(1)}, u32[]{:S(2)}, u32[]{:S(2)}) %collective-permute-start.14) | collective-permute-done | bytes 8224 | tf_op jit(solution)/shard_map/ppermute | solution.py:17
  231.9 0.1 fusion.66
  232.0 14.0 %mul.277 = f32[24576,2]{1,0:T(8,128)} reshape(f32[3,8,16,128]{3,2,1,0:T(8,128)S(1)} %pad_maximum_fusion) | data formatting | bytes 393216 | tf_op jit(solution)/shard_map/mul | solution.py:75
  246.0 7.5 %copy.780 = f32[2,24576]{1,0:T(2,128)S(1)} copy(f32[2,24576]{0,1:T(8,128)} %bitcast.294) | data formatting | bytes 393216 | tf_op jit(solution)/shard_map/mul | solution.py:75
  253.6 0.9 broadcast_multiply_fusion
  254.5 0.5 mul.286
  255.1 0.5 add.165
  255.6 1.9 fusion.85
  257.5 48.6 %psum.14 = f32[8,8]{1,0:T(8,128)S(1)} all-reduce(f32[8,8]{1,0:T(8,128)S(1)} %fusion.85), channel_id=1, replica_groups=mesh['gx'=32,'gy'=16] {'gy'}, use_global_device_ids=true, to_apply=%region_1.0 | all-reduce | flops 64 | bytes 512 | tf_op jit(solution)/shard_map/psum | solution.py:81
  306.1 161.2 %psum.15 = f32[8,8]{1,0:T(8,128)S(1)} all-reduce(f32[8,8]{1,0:T(8,128)S(1)} %psum.14), channel_id=1, replica_groups=mesh['gx'=32,'gy'=16] {'gx'}, use_global_device_ids=true, to_apply=%region_2.0 | all-reduce | flops 64 | bytes 512 | tf_op jit(solution)/shard_map/psum | solution.py:81
  467.3 0.6 broadcast_multiply_fusion.1
  (114 shorter events, 1.2 us)
Async XLA Ops:
  1.4 40.8 %collective-permute-start.1 = (f32[2,1,16,128]{3,2,1,0:T(8,128)S(1)}, f32[2,1,16,128]{3,2,1,0:T(8,128)S(1)}, u32[]{:S(2)}, u32[]{:S(2)}) collective-permute-start(f32[2,1,16,128]{3,2,1,0:T(8,128)S(1)} %slice.390), channel_id=1, source_target_pairs={{0,496},{16,0},{32,16},{48,32},{64,48},{80,64},{96,80},{112,96},{1... | collective-permute-start | bytes 49160 | tf_op jit(solution)/shard_map/ppermute | solution.py:17
  10.1 32.0 %collective-permute-start = (f32[2,8,1,128]{3,1,2,0:T(8,128)S(1)}, f32[2,8,1,128]{3,1,2,0:T(8,128)S(1)}, u32[]{:S(2)}, u32[]{:S(2)}) collective-permute-start(f32[2,8,1,128]{3,1,2,0:T(8,128)S(1)} %pad_maximum_fusion.7), channel_id=1, source_target_pairs={{0,15},{1,0},{2,1},{3,2},{4,3},{5,4},{6,5},{7,6},{8,7},{9,8},{10,9... | collective-permute-start | bytes 24584 | tf_op jit(solution)/shard_map/ppermute | solution.py:17
  20.6 21.6 %copy-start = (f32[3,8,16,128]{3,2,1,0:T(8,128)S(1)}, f32[3,8,16,128]{3,2,1,0:T(8,128)}, u32[]{:S(2)}) copy-start(f32[3,8,16,128]{3,2,1,0:T(8,128)} %param.5) | copy-start | bytes 589828
  20.6 21.8 %copy-start.2 = (f32[3,8,16,128]{3,2,1,0:T(8,128)S(1)}, f32[3,8,16,128]{3,2,1,0:T(8,128)}, u32[]{:S(2)}) copy-start(f32[3,8,16,128]{3,2,1,0:T(8,128)} %param.6) | copy-start | bytes 589828
  42.5 11.6 %collective-permute-start.2 = (f32[2,8,1,128]{3,1,2,0:T(8,128)S(1)}, f32[2,8,1,128]{3,1,2,0:T(8,128)S(1)}, u32[]{:S(2)}, u32[]{:S(2)}) collective-permute-start(f32[2,8,1,128]{3,1,2,0:T(8,128)S(1)} %pad_maximum_fusion.8), channel_id=1, source_target_pairs={{0,1},{1,2},{2,3},{3,4},{4,5},{5,6},{6,7},{7,8},{8,9},{9,10},{10,1... | collective-permute-start | bytes 24584 | tf_op jit(solution)/shard_map/ppermute | solution.py:17
  44.4 14.6 %collective-permute-start.3 = (f32[2,1,16,128]{3,2,1,0:T(8,128)S(1)}, f32[2,1,16,128]{3,2,1,0:T(8,128)S(1)}, u32[]{:S(2)}, u32[]{:S(2)}) collective-permute-start(f32[2,1,16,128]{3,2,1,0:T(8,128)S(1)} %slice.517), channel_id=1, source_target_pairs={{0,16},{16,32},{32,48},{48,64},{64,80},{80,96},{96,112},{112,128},... | collective-permute-start | bytes 49160 | tf_op jit(solution)/shard_map/ppermute | solution.py:17
  59.2 18.3 %collective-permute-start.5 = (f32[2,1,16,128]{3,2,1,0:T(8,128)S(1)}, f32[2,1,16,128]{3,2,1,0:T(8,128)S(1)}, u32[]{:S(2)}, u32[]{:S(2)}) collective-permute-start(f32[2,1,16,128]{3,2,1,0:T(8,128)S(1)} %pad_maximum_fusion.6), channel_id=1, source_target_pairs={{0,496},{16,0},{32,16},{48,32},{64,48},{80,64},{96,80},{112,96},{1... | collective-permute-start | bytes 49160 | tf_op jit(solution)/shard_map/ppermute | solution.py:17
  77.6 29.9 %collective-permute-start.4 = (f32[2,8,1,128]{3,1,2,0:T(8,128)S(1)}, f32[2,8,1,128]{3,1,2,0:T(8,128)S(1)}, u32[]{:S(2)}, u32[]{:S(2)}) collective-permute-start(f32[2,8,1,128]{3,1,2,0:T(8,128)S(1)} %pad_maximum_fusion.9), channel_id=1, source_target_pairs={{0,15},{1,0},{2,1},{3,2},{4,3},{5,4},{6,5},{7,6},{8,7},{9,8},{10,9... | collective-permute-start | bytes 24584 | tf_op jit(solution)/shard_map/ppermute | solution.py:17
  107.7 11.6 %collective-permute-start.6 = (f32[2,8,1,128]{3,1,2,0:T(8,128)S(1)}, f32[2,8,1,128]{3,1,2,0:T(8,128)S(1)}, u32[]{:S(2)}, u32[]{:S(2)}) collective-permute-start(f32[2,8,1,128]{3,1,2,0:T(8,128)S(1)} %pad_maximum_fusion.10), channel_id=1, source_target_pairs={{0,1},{1,2},{2,3},{3,4},{4,5},{5,6},{6,7},{7,8},{8,9},{9,10},{10,1... | collective-permute-start | bytes 24584 | tf_op jit(solution)/shard_map/ppermute | solution.py:17
  109.6 9.6 %collective-permute-start.7 = (f32[2,1,16,128]{3,2,1,0:T(8,128)S(1)}, f32[2,1,16,128]{3,2,1,0:T(8,128)S(1)}, u32[]{:S(2)}, u32[]{:S(2)}) collective-permute-start(f32[2,1,16,128]{3,2,1,0:T(8,128)S(1)} %slice.545), channel_id=1, source_target_pairs={{0,16},{16,32},{32,48},{48,64},{64,80},{80,96},{96,112},{112,128},... | collective-permute-start | bytes 49160 | tf_op jit(solution)/shard_map/ppermute | solution.py:17
  119.5 14.3 %collective-permute-start.9 = (f32[2,1,16,128]{3,2,1,0:T(8,128)S(1)}, f32[2,1,16,128]{3,2,1,0:T(8,128)S(1)}, u32[]{:S(2)}, u32[]{:S(2)}) collective-permute-start(f32[2,1,16,128]{3,2,1,0:T(8,128)S(1)} %pad_maximum_fusion.5), channel_id=1, source_target_pairs={{0,496},{16,0},{32,16},{48,32},{64,48},{80,64},{96,80},{112,96},{1... | collective-permute-start | bytes 49160 | tf_op jit(solution)/shard_map/ppermute | solution.py:17
  133.8 29.9 %collective-permute-start.8 = (f32[2,8,1,128]{3,1,2,0:T(8,128)S(1)}, f32[2,8,1,128]{3,1,2,0:T(8,128)S(1)}, u32[]{:S(2)}, u32[]{:S(2)}) collective-permute-start(f32[2,8,1,128]{3,1,2,0:T(8,128)S(1)} %pad_maximum_fusion.11), channel_id=1, source_target_pairs={{0,15},{1,0},{2,1},{3,2},{4,3},{5,4},{6,5},{7,6},{8,7},{9,8},{10,9... | collective-permute-start | bytes 24584 | tf_op jit(solution)/shard_map/ppermute | solution.py:17
  164.0 11.6 %collective-permute-start.10 = (f32[2,8,1,128]{3,1,2,0:T(8,128)S(1)}, f32[2,8,1,128]{3,1,2,0:T(8,128)S(1)}, u32[]{:S(2)}, u32[]{:S(2)}) collective-permute-start(f32[2,8,1,128]{3,1,2,0:T(8,128)S(1)} %pad_maximum_fusion.12), channel_id=1, source_target_pairs={{0,1},{1,2},{2,3},{3,4},{4,5},{5,6},{6,7},{7,8},{8,9},{9,10},{10,1... | collective-permute-start | bytes 24584 | tf_op jit(solution)/shard_map/ppermute | solution.py:17
  165.9 9.6 %collective-permute-start.11 = (f32[2,1,16,128]{3,2,1,0:T(8,128)S(1)}, f32[2,1,16,128]{3,2,1,0:T(8,128)S(1)}, u32[]{:S(2)}, u32[]{:S(2)}) collective-permute-start(f32[2,1,16,128]{3,2,1,0:T(8,128)S(1)} %slice.573), channel_id=1, source_target_pairs={{0,16},{16,32},{32,48},{48,64},{64,80},{80,96},{96,112},{112,128},... | collective-permute-start | bytes 49160 | tf_op jit(solution)/shard_map/ppermute | solution.py:17
  175.7 14.3 %collective-permute-start.13 = (f32[2,1,16,128]{3,2,1,0:T(8,128)S(1)}, f32[2,1,16,128]{3,2,1,0:T(8,128)S(1)}, u32[]{:S(2)}, u32[]{:S(2)}) collective-permute-start(f32[2,1,16,128]{3,2,1,0:T(8,128)S(1)} %pad_maximum_fusion.4), channel_id=1, source_target_pairs={{0,496},{16,0},{32,16},{48,32},{64,48},{80,64},{96,80},{112,96},{1... | collective-permute-start | bytes 49160 | tf_op jit(solution)/shard_map/ppermute | solution.py:17
  190.1 29.9 %collective-permute-start.12 = (f32[2,8,1,128]{3,1,2,0:T(8,128)S(1)}, f32[2,8,1,128]{3,1,2,0:T(8,128)S(1)}, u32[]{:S(2)}, u32[]{:S(2)}) collective-permute-start(f32[2,8,1,128]{3,1,2,0:T(8,128)S(1)} %pad_maximum_fusion.13), channel_id=1, source_target_pairs={{0,15},{1,0},{2,1},{3,2},{4,3},{5,4},{6,5},{7,6},{8,7},{9,8},{10,9... | collective-permute-start | bytes 24584 | tf_op jit(solution)/shard_map/ppermute | solution.py:17
  220.2 33.4 %copy-start.1 = (f32[3,8,16,128]{3,2,1,0:T(8,128)}, f32[3,8,16,128]{3,2,1,0:T(8,128)S(1)}, u32[]{:S(2)}) copy-start(f32[3,8,16,128]{3,2,1,0:T(8,128)S(1)} %fusion.3) | copy-start | bytes 589828
  220.2 11.6 %collective-permute-start.14 = (f32[2,8,1,128]{3,1,2,0:T(8,128)S(1)}, f32[2,8,1,128]{3,1,2,0:T(8,128)S(1)}, u32[]{:S(2)}, u32[]{:S(2)}) collective-permute-start(f32[2,8,1,128]{3,1,2,0:T(8,128)S(1)} %pad_maximum_fusion.14), channel_id=1, source_target_pairs={{0,1},{1,2},{2,3},{3,4},{4,5},{5,6},{6,7},{7,8},{8,9},{9,10},{10,1... | collective-permute-start | bytes 24584 | tf_op jit(solution)/shard_map/ppermute | solution.py:17
  222.2 9.6 %collective-permute-start.15 = (f32[2,1,16,128]{3,2,1,0:T(8,128)S(1)}, f32[2,1,16,128]{3,2,1,0:T(8,128)S(1)}, u32[]{:S(2)}, u32[]{:S(2)}) collective-permute-start(f32[2,1,16,128]{3,2,1,0:T(8,128)S(1)} %slice.602), channel_id=1, source_target_pairs={{0,16},{16,32},{32,48},{48,64},{64,80},{80,96},{96,112},{112,128},... | collective-permute-start | bytes 49160 | tf_op jit(solution)/shard_map/ppermute | solution.py:17
  232.0 21.6 %copy-start.3 = (f32[3,8,16,128]{3,2,1,0:T(8,128)}, f32[3,8,16,128]{3,2,1,0:T(8,128)S(1)}, u32[]{:S(2)}) copy-start(f32[3,8,16,128]{3,2,1,0:T(8,128)S(1)} %pad_maximum_fusion) | copy-start | bytes 589828
